TPU v7x, 32 devices: a whole 2x2x4 slice. The times are simulated.
32 devices in a mesh: groups: 2 (over y), row: 4 (over z), col: 4 (over x, core).
Axes of the slice: x: 2, y: 2, z: 4, core: 2. Of those that a mesh axis runs over, the one named last changes fastest.
Arguments:
- patches: bfloat16 [8, 4, 1024, 1408], P(('groups', 'row'), 'col'), parts along dimension 0, may hold values from -54 to 54
- keep_list: int32 [8, 4, 256], P(('groups', 'row'), 'col'), parts along dimension 0, may hold values from 0 to 1023, as said below
- destination: int32 [8, 4, 256], P(('groups', 'row'), 'col'), parts along dimension 0, may hold values from -1 to 255, as said below
- counts: int32 [8, 4], P('groups'), parts along dimension 0, may hold values from 64 to 256, as said below
- link_open: int32 [8, 4, 2], P('groups'), parts along dimension 0, may hold values 0 or 1
- ln_gain: float32 [1408], replicated, may hold values from 0.1 to 1.9
- w_qkv: bfloat16 [1408, 2112], replicated, may hold values from -0.15625 to 0.15625
- head_scale: float32 [8], replicated, may hold values from 1 to 4
- w_out: bfloat16 [704, 1408], replicated, may hold values from -0.4375 to 0.4375
- cotangent: bfloat16 [8, 4, 256, 1408], P(('groups', 'row'), 'col'), parts along dimension 0, may hold values from -6 to 6
Outputs:
- layer_out: bfloat16 [8, 4, 256, 1408], P(('groups', 'row'), 'col'), parts along dimension 0
- patch_grad: bfloat16 [8, 4, 256, 1408], P(('groups', 'row'), 'col'), parts along dimension 0
There are 2 independent parts, one for each index of `groups`. A program takes and returns all parts, laid end to end along the dimension named above; an argument that names none is the same for every part. Nothing has to cross between parts.
Inputs may be any that keep to these rules, and one draw needn't show every extreme that they name: `keep_list`: within a window the entries are distinct patch indices. `counts`: some window keeps 256 tokens. destination[r, c, j] is -1 exactly where j >= counts[r, c]; elsewhere the owner along row is destination // 64 and the position in the window's block is destination % 64; entries of one window are distinct, so a window sends at most 64 tokens to one owner, and in every column some owner receives 64 tokens from every window.
All inputs are finite; a program needn't handle non-finite values.
Results may differ from a plain program's by a relative error of at most 0.012.
The roundings to bfloat16 on the way count: a program that leaves them out, or rounds other values in their place, can miss the bound.
Values may be sent and summed in bfloat16 or wider, within the bound.
A program may use at most 128 MiB of HBM per device.

v0:
```python
import math

import jax
import jax.numpy as jnp
from jax import lax
from jax.sharding import PartitionSpec as P

D = 1408
HEADS = 8
HEAD_DIM = 88
KEEP = 256


def extended_2(block, sides, width):
    for axis, dim in sides:
        count = lax.axis_size(axis)
        forward = [(i, i + 1) for i in range(count - 1)]
        backward = [(target, source) for source, target in forward]
        low = lax.ppermute(
            lax.slice_in_dim(block, block.shape[dim] - width, None, axis=dim), axis, forward
        )
        high = lax.ppermute(lax.slice_in_dim(block, 0, width, axis=dim), axis, backward)
        block = jnp.concatenate([low, block, high], axis=dim)
    return block


def layer_norm(kept_rows, ln_gain):
    values = kept_rows.astype(jnp.float32)
    center = jnp.mean(values, axis=-1, keepdims=True)
    centred = values - center
    spread = jnp.mean(centred * centred, axis=-1, keepdims=True)
    inv_std = lax.rsqrt(spread + 1e-06)
    scaled = centred * inv_std
    return ((scaled * ln_gain).astype(jnp.bfloat16), scaled, inv_std)


def head_norm(raw_rows):
    row_count = raw_rows.shape[0]
    split_heads = raw_rows.reshape(row_count, HEADS, HEAD_DIM)
    inv_rms = lax.rsqrt(jnp.mean(split_heads * split_heads, axis=-1, keepdims=True) + 1e-06)
    return ((split_heads * inv_rms).astype(jnp.bfloat16), split_heads, inv_rms)


def head_norm_back(split_heads, inv_rms, upstream):
    inner_mean = jnp.mean(upstream * split_heads, axis=-1, keepdims=True)
    return inv_rms * (upstream - split_heads * inv_rms * inv_rms * inner_mean)


def attend(queries, key_rows, value_rows, key_valid, score_coef):
    scores = (
        jnp.einsum("qhe,khe->hqk", queries, key_rows, preferred_element_type=jnp.float32)
        * score_coef[:, None, None]
    )
    raised = jnp.where(key_valid[None, None, :], jnp.exp(scores), 0.0)
    total_sum = jnp.sum(raised, axis=-1, keepdims=True)
    weights = raised / total_sum
    rounded = weights.astype(jnp.bfloat16)
    attended = jnp.einsum("hqk,khe->qhe", rounded, value_rows, preferred_element_type=jnp.float32)
    return (attended.astype(jnp.bfloat16), weights, rounded, total_sum)


def score_back(weights, value_rows, out_grad):
    dot_grad = jnp.einsum("qhe,khe->hqk", out_grad, value_rows, preferred_element_type=jnp.float32)
    row_delta = jnp.sum(weights * dot_grad, axis=-1, keepdims=True)
    return ((weights * (dot_grad - row_delta)).astype(jnp.bfloat16), row_delta)


def query_back(score_grad, key_rows, score_coef):
    return (
        jnp.einsum("hqk,khe->qhe", score_grad, key_rows, preferred_element_type=jnp.float32)
        * score_coef[None, :, None]
    )


def key_back(score_grad, rounded, queries, out_grad, score_coef):
    key_part = (
        jnp.einsum("hqk,qhe->khe", score_grad, queries, preferred_element_type=jnp.float32)
        * score_coef[None, :, None]
    )
    value_part = jnp.einsum("hqk,qhe->khe", rounded, out_grad, preferred_element_type=jnp.float32)
    return (key_part, value_part)


def per_device(
    patches, keep_list, destination, counts, link_open, ln_gain, w_qkv, head_scale, w_out, cotangent
):
    row_at = lax.axis_index("row")
    col_at = lax.axis_index("col")
    row_total = lax.axis_size("row")
    col_total = lax.axis_size("col")
    width = HEADS * HEAD_DIM
    slot_cap = KEEP // row_total
    head_shape = (KEEP, HEADS, HEAD_DIM)
    kept_rows = patches[0, 0][keep_list[0, 0]]
    normed, scaled, inv_std = layer_norm(kept_rows, ln_gain)
    projected = jnp.dot(normed, w_qkv, preferred_element_type=jnp.float32)
    query_norm, query_split, query_rms = head_norm(projected[:, :width])
    key_norm, key_split, key_rms = head_norm(projected[:, width : 2 * width])
    value_rows = projected[:, 2 * width :].astype(jnp.bfloat16)
    value_heads = value_rows.reshape(head_shape)
    score_coef = head_scale / math.sqrt(HEAD_DIM)
    position = jnp.arange(KEEP)
    above_row = jnp.maximum(row_at - 1, 0)
    below_row = jnp.minimum(row_at + 1, row_total - 1)
    left_col = jnp.maximum(col_at - 1, 0)
    right_col = jnp.minimum(col_at + 1, col_total - 1)
    above_open = (row_at > 0) & (link_open[above_row, col_at, 1] == 1)
    below_open = (row_at < row_total - 1) & (link_open[row_at, col_at, 1] == 1)
    left_open = (col_at > 0) & (link_open[row_at, left_col, 0] == 1)
    right_open = (col_at < col_total - 1) & (link_open[row_at, col_at, 0] == 1)
    open_list = [above_open, below_open, left_open, right_open]
    own_valid = position < counts[row_at, col_at]
    key_valid = jnp.concatenate(
        [
            own_valid,
            (position < counts[above_row, col_at]) & above_open,
            (position < counts[below_row, col_at]) & below_open,
            (position < counts[row_at, left_col]) & left_open,
            (position < counts[row_at, right_col]) & right_open,
        ],
        axis=0,
    )
    live_slot = destination[0, 0] >= 0
    safe_slot = jnp.maximum(destination[0, 0], 0)
    incoming = lax.all_to_all(
        cotangent[0, 0].reshape(row_total, slot_cap, D),
        "row",
        split_axis=0,
        concat_axis=0,
        tiled=True,
    ).reshape(KEEP, D)
    token_grad = jnp.where(live_slot[:, None], incoming[safe_slot], 0.0)
    out_grad = (
        jnp.dot(token_grad, w_out.T, preferred_element_type=jnp.float32)
        .astype(jnp.bfloat16)
        .reshape(head_shape)
    )
    own_keys = key_norm.reshape(KEEP, width)
    grid_places = ((0, 1), (2, 1), (1, 0), (1, 2))
    panel = jnp.concatenate([query_norm.reshape(KEEP, width), own_keys, value_rows], axis=1)[
        None, None
    ]
    extended = extended_2(panel, (("row", 0), ("col", 1)), 1)
    stacked = jnp.concatenate(
        [panel[0, 0, :, width:]]
        + [extended[grid_row, grid_col][:, width:] for grid_row, grid_col in grid_places],
        axis=0,
    )
    key_rows = stacked[:, :width].reshape(5 * KEEP, HEADS, HEAD_DIM)
    value_all = stacked[:, width:].reshape(5 * KEEP, HEADS, HEAD_DIM)
    attended, weights, rounded, total_sum = attend(
        query_norm, key_rows, value_all, key_valid, score_coef
    )
    score_grad, row_delta = score_back(weights, value_all, out_grad)
    query_part = query_back(score_grad, key_rows, score_coef)
    key_acc, value_acc = key_back(
        score_grad[:, :, :KEEP], rounded[:, :, :KEEP], query_norm, out_grad, score_coef
    )
    grad_ext = extended_2(out_grad.reshape(KEEP, width)[None, None], (("row", 0), ("col", 1)), 1)
    stats = jnp.stack([total_sum[..., 0], row_delta[..., 0]])[None, None]
    stats_ext = extended_2(stats, (("row", 0), ("col", 1)), 1)
    for which, (grid_row, grid_col) in enumerate(grid_places):
        far_queries = extended[grid_row, grid_col][:, :width].reshape(head_shape)
        far_grad = grad_ext[grid_row, grid_col].reshape(head_shape)
        far_total = stats_ext[grid_row, grid_col, 0][..., None]
        far_delta = stats_ext[grid_row, grid_col, 1][..., None]
        scores = (
            jnp.einsum("qhe,khe->hqk", far_queries, key_norm, preferred_element_type=jnp.float32)
            * score_coef[:, None, None]
        )
        raised = jnp.where((own_valid & open_list[which])[None, None, :], jnp.exp(scores), 0.0)
        safe_total = jnp.where(far_total > 0, far_total, 1.0)
        far_weights = raised / safe_total
        far_rounded = far_weights.astype(jnp.bfloat16)
        dot_grad = jnp.einsum(
            "qhe,khe->hqk", far_grad, value_heads, preferred_element_type=jnp.float32
        )
        far_score = (far_weights * (dot_grad - far_delta)).astype(jnp.bfloat16)
        key_more, value_more = key_back(far_score, far_rounded, far_queries, far_grad, score_coef)
        key_acc = key_acc + key_more
        value_acc = value_acc + value_more
    key_value_grad = jnp.concatenate(
        [key_acc.reshape(KEEP, width), value_acc.reshape(KEEP, width)], axis=-1
    )
    kept_out = (
        kept_rows.astype(jnp.float32)
        + jnp.dot(attended.reshape(KEEP, width), w_out, preferred_element_type=jnp.float32)
    ).astype(jnp.bfloat16)
    target_slot = jnp.where(live_slot, destination[0, 0], KEEP)
    outgoing = jnp.zeros((KEEP, D), jnp.bfloat16).at[target_slot].set(kept_out, mode="drop")
    layer_out = lax.all_to_all(
        outgoing.reshape(row_total, slot_cap, D), "row", split_axis=0, concat_axis=0, tiled=True
    ).reshape(KEEP, D)
    query_pre = head_norm_back(query_split, query_rms, query_part)
    key_pre = head_norm_back(key_split, key_rms, key_value_grad[:, :width].reshape(head_shape))
    proj_grad = jnp.concatenate(
        [query_pre.reshape(KEEP, width), key_pre.reshape(KEEP, width), key_value_grad[:, width:]],
        axis=1,
    ).astype(jnp.bfloat16)
    normed_grad = jnp.dot(proj_grad, w_qkv.T, preferred_element_type=jnp.float32)
    gained = normed_grad * ln_gain
    back_norm = inv_std * (
        gained
        - jnp.mean(gained, axis=-1, keepdims=True)
        - scaled * jnp.mean(gained * scaled, axis=-1, keepdims=True)
    )
    patch_grad = (token_grad.astype(jnp.float32) + back_norm).astype(jnp.bfloat16)
    return (layer_out[None, None], patch_grad[None, None])


def solution(mesh):
    placed = (
        P(("groups", "row"), "col", None, None),
        P(("groups", "row"), "col", None),
        P(("groups", "row"), "col", None),
        P("groups", None),
        P("groups", None, None),
        P(),
        P(),
        P(),
        P(),
        P(("groups", "row"), "col", None, None),
    )
    return jax.shard_map(
        per_device,
        mesh=mesh,
        in_specs=placed,
        out_specs=(
            P(("groups", "row"), "col", None, None),
            P(("groups", "row"), "col", None, None),
        ),
        check_vma=False,
    )
```

profile of v0, /device:TPU:14, one launch (start us, length us, event | category | flops | bytes accessed | tf_op | source)
XLA Modules:
  0.0 194.7 jit_solution(17263657993999506515)
XLA Ops:
  2.5 2.1 %gather_fusion = bf16[256,1408]{1,0:T(8,128)(2,1)} fusion(bf16[1024,1408]{1,0:T(8,128)(2,1)S(1)} %bitcast.136, s32[1024]{0:T(1024)S(1)} %get-tuple-element.33), kind=kCustom, calls=%fused_computation | custom fusion | bytes 1442816 | tf_op jit(solution)/shard_map/gather | solution.py:94
  7.3 5.0 %fusion.49 = f32[256,2112]{0,1:T(8,128)S(1)} fusion(bf16[1408,2112]{0,1:T(8,128)(2,1)} %param.16, bf16[256,1408]{1,0:T(8,128)(2,1)} %gather_fusion, f32[1408]{0:T(1024)S(1)} %copy-done.29, f32[256]{0:T(256)S(1)} %add_rsqrt_fusion.2, f32[256]{0:T(256)S(1)} %broadcast_multiply_fusion.4), kind=kOutput, calls=%fused_computation.77 | convolution fusion | flops 1524334592 | bytes 8838656 | tf_op jit(solution)/shard_map/dot_general | solution.py:96
  13.9 3.5 %collective-permute-start = (bf16[1,1,256,2112]{2,3,1,0:T(8,128)(2,1)}, bf16[1,1,256,2112]{2,3,1,0:T(8,128)(2,1)}, u32[]{:S(2)}, u32[]{:S(2)}) collective-permute-start(bf16[1,1,256,2112]{2,3,1,0:T(8,128)(2,1)} %maximum_bitcast_fusion), channel_id=1, source_target_pairs={{0,4},{4,8},{8,12},{1,5},{5,9},{9,13},{2,6},{6,10},{10,14},{3,7},{... | collective-permute-start | bytes 3244040 | tf_op jit(solution)/shard_map/ppermute | solution.py:19
  17.4 3.4 %collective-permute-start.1 = (bf16[1,1,256,2112]{2,3,1,0:T(8,128)(2,1)}, bf16[1,1,256,2112]{2,3,1,0:T(8,128)(2,1)}, u32[]{:S(2)}, u32[]{:S(2)}) collective-permute-start(bf16[1,1,256,2112]{2,3,1,0:T(8,128)(2,1)} %maximum_bitcast_fusion), channel_id=1, source_target_pairs={{4,0},{8,4},{12,8},{5,1},{9,5},{13,9},{6,2},{10,6},{14,10},{7,3},{... | collective-permute-start | bytes 3244040 | tf_op jit(solution)/shard_map/ppermute | solution.py:22
  20.8 5.3 %all-to-all-start.1 = ((bf16[4,64,1408]{2,1,0:T(8,128)(2,1)}), bf16[4,64,1408]{2,1,0:T(8,128)(2,1)S(1)}, u32[]{:S(2)}, u32[]{:S(2)}) async-start(bf16[4,64,1408]{2,1,0:T(8,128)(2,1)} %bitcast.30), calls=%async_computation.1 | async-start | bytes 1441792 | tf_op jit(solution)/shard_map/all_to_all | solution.py:125
  33.4 9.4 %collective-permute-done = bf16[1,1,256,2112]{2,3,1,0:T(8,128)(2,1)} collective-permute-done((bf16[1,1,256,2112]{2,3,1,0:T(8,128)(2,1)}, bf16[1,1,256,2112]{2,3,1,0:T(8,128)(2,1)}, u32[]{:S(2)}, u32[]{:S(2)}) %collective-permute-start) | collective-permute-done | bytes 1081376 | tf_op jit(solution)/shard_map/ppermute | solution.py:19
  42.9 6.4 %collective-permute-done.1 = bf16[1,1,256,2112]{2,3,1,0:T(8,128)(2,1)} collective-permute-done((bf16[1,1,256,2112]{2,3,1,0:T(8,128)(2,1)}, bf16[1,1,256,2112]{2,3,1,0:T(8,128)(2,1)}, u32[]{:S(2)}, u32[]{:S(2)}) %collective-permute-start.1) | collective-permute-done | bytes 1081376 | tf_op jit(solution)/shard_map/ppermute | solution.py:22
  49.2 3.9 %pad_maximum_fusion = bf16[3,1,256,2112]{2,3,1,0:T(8,128)(2,1)} fusion(bf16[1,1,256,2112]{2,3,1,0:T(8,128)(2,1)} %collective-permute-done.1, bf16[1,1,256,2112]{2,3,1,0:T(8,128)(2,1)} %maximum_bitcast_fusion, bf16[1,1,256,2112]{2,3,1,0:T(8,128)(2,1)} %collective-permute-done), kind=kLoop, calls=%fused_computation.8 | loop fusion | flops 3244032 | bytes 6488064 | tf_op jit(solution)/shard_map/concatenate | solution.py:23
  58.7 4.2 %collective-permute-start.2 = (bf16[3,1,256,2112]{2,3,1,0:T(8,128)(2,1)}, bf16[3,1,256,2112]{2,3,1,0:T(8,128)(2,1)}, u32[]{:S(2)}, u32[]{:S(2)}) collective-permute-start(bf16[3,1,256,2112]{2,3,1,0:T(8,128)(2,1)} %pad_maximum_fusion), channel_id=1, source_target_pairs={{0,1},{1,2},{2,3},{4,5},{5,6},{6,7},{8,9},{9,10},{10,11},{12,13},{... | collective-permute-start | bytes 9732104 | tf_op jit(solution)/shard_map/ppermute | solution.py:19
  65.8 2.6 %convolution_convert_fusion.1 = bf16[256,704]{0,1:T(8,128)(2,1)S(1)} fusion(bf16[704,1408]{1,0:T(8,128)(2,1)} %param.18, bf16[256,1408]{1,0:T(8,128)(2,1)} %gather_fusion.1, pred[256]{0:T(512)(128)(4,1)S(1)} %compare_reduce_fusion), kind=kOutput, calls=%fused_computation.52 | convolution fusion | flops 508051456 | bytes 3064064 | tf_op jit(solution)/shard_map/dot_general | solution.py:134
  68.4 3.4 %collective-permute-start.7 = (bf16[1,1,256,704]{2,3,1,0:T(8,128)(2,1)S(1)}, bf16[1,1,256,704]{2,3,1,0:T(8,128)(2,1)S(1)}, u32[]{:S(2)}, u32[]{:S(2)}) collective-permute-start(bf16[1,1,256,704]{2,3,1,0:T(8,128)(2,1)S(1)} %bitcast.165), channel_id=1, source_target_pairs={{4,0},{8,4},{12,8},{5,1},{9,5},{13,9},{6,2},{10,6},{14,10},{7,3},{... | collective-permute-start | bytes 1081352 | tf_op jit(solution)/shard_map/ppermute | solution.py:22
  71.8 2.5 %collective-permute-start.5 = (bf16[1,1,256,704]{2,3,1,0:T(8,128)(2,1)S(1)}, bf16[1,1,256,704]{2,3,1,0:T(8,128)(2,1)S(1)}, u32[]{:S(2)}, u32[]{:S(2)}) collective-permute-start(bf16[1,1,256,704]{2,3,1,0:T(8,128)(2,1)S(1)} %bitcast.166), channel_id=1, source_target_pairs={{0,4},{4,8},{8,12},{1,5},{5,9},{9,13},{2,6},{6,10},{10,14},{3,7},{... | collective-permute-start | bytes 1081352 | tf_op jit(solution)/shard_map/ppermute | solution.py:19
  80.0 3.1 %collective-permute-done.5 = bf16[1,1,256,704]{2,3,1,0:T(8,128)(2,1)S(1)} collective-permute-done((bf16[1,1,256,704]{2,3,1,0:T(8,128)(2,1)S(1)}, bf16[1,1,256,704]{2,3,1,0:T(8,128)(2,1)S(1)}, u32[]{:S(2)}, u32[]{:S(2)}) %collective-permute-start.5) | collective-permute-done | bytes 360480 | tf_op jit(solution)/shard_map/ppermute | solution.py:19
  85.1 2.7 %collective-permute-start.9 = (bf16[3,1,256,704]{2,3,1,0:T(8,128)(2,1)S(1)}, bf16[3,1,256,704]{2,3,1,0:T(8,128)(2,1)S(1)}, u32[]{:S(2)}, u32[]{:S(2)}) collective-permute-start(bf16[3,1,256,704]{2,3,1,0:T(8,128)(2,1)S(1)} %pad_maximum_fusion.1), channel_id=1, source_target_pairs={{0,1},{1,2},{2,3},{4,5},{5,6},{6,7},{8,9},{9,10},{10,11},{12,13},{... | collective-permute-start | bytes 3244040 | tf_op jit(solution)/shard_map/ppermute | solution.py:19
  91.9 10.7 %collective-permute-done.11 = bf16[3,1,256,704]{2,3,1,0:T(8,128)(2,1)S(1)} collective-permute-done((bf16[3,1,256,704]{2,3,1,0:T(8,128)(2,1)S(1)}, bf16[3,1,256,704]{2,3,1,0:T(8,128)(2,1)S(1)}, u32[]{:S(2)}, u32[]{:S(2)}) %collective-permute-start.11) | collective-permute-done | bytes 1081376 | tf_op jit(solution)/shard_map/ppermute | solution.py:22
  103.5 6.7 %collective-permute-done.9 = bf16[3,1,256,704]{2,3,1,0:T(8,128)(2,1)S(1)} collective-permute-done((bf16[3,1,256,704]{2,3,1,0:T(8,128)(2,1)S(1)}, bf16[3,1,256,704]{2,3,1,0:T(8,128)(2,1)S(1)}, u32[]{:S(2)}, u32[]{:S(2)}) %collective-permute-start.9) | collective-permute-done | bytes 1081376 | tf_op jit(solution)/shard_map/ppermute | solution.py:19
  114.6 2.5 %fusion.1 = (f32[8,256]{1,0:T(8,128)S(1)}, f32[8,256,1280]{2,1,0:T(8,128)S(1)}) fusion(f32[8]{0:T(128)S(1)} %broadcast_multiply_fusion.5, pred[1280]{0:T(1024)(128)(4,1)S(1)} %constant_dynamic-update-slice_fusion, bf16[1280,8,88]{0,2,1:T(8,128)(2,1)S(1)} %bitcast.149, f32[256,8,88]{0,2,1:T(8,128)S(1)} %bitcast.139, f32[256,8]{0,1:T(8,128)S(1)} %add_rsqrt_fusion.1), kind=kOutput, calls=%fused_computation.7 | convolution fusion | flops 469596160 | bytes 13026592 | tf_op jit(solution)/shard_map/qhe,khe->hqk/dot_general | solution.py:51
  117.2 5.9 %multiply_reduce_fusion = (f32[8,256]{1,0:T(8,128)S(1)}, f32[8,256,1280]{2,1,0:T(8,128)}) fusion(f32[8,256]{1,0:T(8,128)S(1)} %get-tuple-element.23, f32[8,256,1280]{2,1,0:T(8,128)S(1)} %get-tuple-element.24, f32[8]{0:T(128)S(1)} %broadcast_multiply_fusion.5, pred[1280]{0:T(1024)(128)(4,1)S(1)} %constant_dynamic-update-slice_fusion, ...), kind=kOutput, calls=%fused_computation.4 | convolution fusion | flops 474478592 | bytes 23151904 | tf_op jit(solution)/shard_map/qhe,khe->hqk/dot_general | solution.py:63
  123.1 3.4 %collective-permute-start.6 = (f32[1,1,2,8,256]{4,3,2,1,0:T(8,128)S(1)}, f32[1,1,2,8,256]{4,3,2,1,0:T(8,128)S(1)}, u32[]{:S(2)}, u32[]{:S(2)}) collective-permute-start(f32[1,1,2,8,256]{4,3,2,1,0:T(8,128)S(1)} %maximum_bitcast_fusion.1), channel_id=1, source_target_pairs={{4,0},{8,4},{12,8},{5,1},{9,5},{13,9},{6,2},{10,6},{14,10},{7,3},{... | collective-permute-start | bytes 49160 | tf_op jit(solution)/shard_map/ppermute | solution.py:22
  126.5 2.5 %collective-permute-start.4 = (f32[1,1,2,8,256]{4,3,2,1,0:T(8,128)S(1)}, f32[1,1,2,8,256]{4,3,2,1,0:T(8,128)S(1)}, u32[]{:S(2)}, u32[]{:S(2)}) collective-permute-start(f32[1,1,2,8,256]{4,3,2,1,0:T(8,128)S(1)} %maximum_bitcast_fusion.1), channel_id=1, source_target_pairs={{0,4},{4,8},{8,12},{1,5},{5,9},{9,13},{2,6},{6,10},{10,14},{3,7},{... | collective-permute-start | bytes 49160 | tf_op jit(solution)/shard_map/ppermute | solution.py:19
  129.7 6.1 %multiply_convert_fusion = (bf16[8,256,1280]{2,1,0:T(8,128)(2,1)S(1)}, bf16[8,256,1280]{2,1,0:T(8,128)(2,1)S(1)}) fusion(f32[8,256,1280]{2,1,0:T(8,128)} %get-tuple-element.26, f32[8,256]{1,0:T(8,128)S(1)} %get-tuple-element.25, f32[8,256]{1,0:T(8,128)S(1)} %get-tuple-element.23, f32[8,256,1280]{2,1,0:T(8,128)S(1)} %get-tuple-element.24, ...), kind=kLoop, calls=%fused_computation.3 | loop fusion | flops 18350080 | bytes 31474976 | tf_op jit(solution)/shard_map/convert_element_type | solution.py:65
  139.9 2.6 %multiply_reduce_fusion.2 = (f32[256,8]{0,1:T(8,128)S(1)}, f32[256,8,88]{0,2,1:T(8,128)}) fusion(f32[256,8,88]{0,2,1:T(8,128)S(1)} %bitcast.141, f32[8]{0:T(128)S(1)} %broadcast_multiply_fusion.5, bf16[1280,8,88]{0,2,1:T(8,128)(2,1)S(1)} %bitcast.150, bf16[8,256,1280]{2,1,0:T(8,128)(2,1)S(1)} %get-tuple-element.4), kind=kOutput, calls=%fused_computation.92 | convolution fusion | flops 461912064 | bytes 8495136 | tf_op jit(solution)/shard_map/hqk,khe->qhe/dot_general | solution.py:70
  144.2 3.2 %scatter_custom_fusion = bf16[256,1408]{1,0:T(8,128)(2,1)} fusion(s32[256]{0:T(256)S(1)} %bitcast.184, bf16[256,1408]{1,0:T(8,128)(2,1)} %fusion.2, bf16[]{:T(256)} %constant.41.clone.1), kind=kCustom, calls=%fused_computation.101 | custom fusion | bytes 721408 | tf_op jit(solution)/shard_map/scatter | solution.py:190
  147.4 5.6 %all-to-all-start = ((bf16[4,64,1408]{2,1,0:T(8,128)(2,1)}), bf16[4,64,1408]{2,1,0:T(8,128)(2,1)}, u32[]{:S(2)}, u32[]{:S(2)}) async-start(bf16[4,64,1408]{2,1,0:T(8,128)(2,1)} %bitcast.151), calls=%async_computation | async-start | bytes 1441792 | tf_op jit(solution)/shard_map/all_to_all | solution.py:191
  159.5 2.6 %collective-permute-start.8 = (f32[3,1,2,8,256]{4,3,2,1,0:T(8,128)S(1)}, f32[3,1,2,8,256]{4,3,2,1,0:T(8,128)S(1)}, u32[]{:S(2)}, u32[]{:S(2)}) collective-permute-start(f32[3,1,2,8,256]{4,3,2,1,0:T(8,128)S(1)} %pad_maximum_fusion.2), channel_id=1, source_target_pairs={{0,1},{1,2},{2,3},{4,5},{5,6},{6,7},{8,9},{9,10},{10,11},{12,13},{... | collective-permute-start | bytes 147464 | tf_op jit(solution)/shard_map/ppermute | solution.py:19
  163.8 3.7 %fusion.24 = f32[8,88,256]{2,1,0:T(8,128)} fusion(f32[8,88,256]{2,1,0:T(8,128)} %fusion.36, bf16[256,8,88]{0,2,1:T(8,128)(2,1)S(1)} %bitcast.160, bf16[256,8,88]{0,2,1:T(8,128)(2,1)S(1)} %bitcast.179, bf16[256,8,88]{0,2,1:T(8,128)(2,1)S(1)} %bitcast.153, f32[8,256]{1,0:T(8,128)S(1)} %slice_bitcast_fusion.9, f32[8,256,256]{2,1,0:T(8,128)} %fusion.75, ...), kind=kOutput, calls=%fused_computation.43 | convolution fusion | flops 187875328 | bytes 4636960 | tf_op jit(solution)/shard_map/hqk,qhe->khe/dot_general | solution.py:77
  167.6 3.6 %fusion.18 = f32[8,88,256]{2,1,0:T(8,128)} fusion(bf16[256,8,88]{0,2,1:T(8,128)(2,1)S(1)} %bitcast.162, bf16[256,8,88]{0,2,1:T(8,128)(2,1)S(1)} %bitcast.174, bf16[256,8,88]{0,2,1:T(8,128)(2,1)S(1)} %bitcast.154, f32[8,256]{1,0:T(8,128)S(1)} %slice_bitcast_fusion.3, f32[8,256,256]{2,1,0:T(8,128)} %fusion.78, f32[8,256]{1,0:T(8,128)S(1)} %compare_select_fusion, ...), kind=kOutput, calls=%fused_computation.37 | convolution fusion | flops 187695104 | bytes 3916064 | tf_op jit(solution)/shard_map/hqk,qhe->khe/dot_general | solution.py:77
  171.2 3.3 %fusion.38 = f32[8,88,256]{2,1,0:T(8,128)} fusion(bf16[256,8,88]{0,2,1:T(8,128)(2,1)S(1)} %bitcast.175, f32[8,256,256]{2,1,0:T(8,128)} %fusion.78, f32[8,256]{1,0:T(8,128)S(1)} %compare_select_fusion, f32[8]{0:T(128)S(1)} %broadcast_multiply_fusion.5, pred[256]{0:T(512)(128)(4,1)S(1)} %get-tuple-element.34), kind=kOutput, calls=%fused_computation.66 | convolution fusion | flops 94371840 | bytes 3186976 | tf_op jit(solution)/shard_map/hqk,qhe->khe/dot_general | solution.py:80
  176.0 3.5 %fusion.17 = f32[8,88,256]{2,1,0:T(8,128)} fusion(bf16[256,8,88]{0,2,1:T(8,128)(2,1)S(1)} %bitcast.164, bf16[256,8,88]{0,2,1:T(8,128)(2,1)S(1)} %bitcast.173, bf16[256,8,88]{0,2,1:T(8,128)(2,1)S(1)} %bitcast.155, f32[8,256]{1,0:T(8,128)S(1)} %slice_bitcast_fusion.5, f32[8,256,256]{2,1,0:T(8,128)} %fusion.77, f32[8,256]{1,0:T(8,128)S(1)} %compare_select_fusion.1, ...), kind=kOutput, calls=%fused_computation.36 | convolution fusion | flops 187695104 | bytes 3916064 | tf_op jit(solution)/shard_map/hqk,qhe->khe/dot_general | solution.py:77
  179.6 3.4 %multiply_reduce_fusion.1 = (f32[256,8]{0,1:T(8,128)S(1)}, f32[256,8,88]{0,2,1:T(8,128)S(1)}) fusion(f32[256,8,88]{0,2,1:T(8,128)S(1)} %bitcast.145, f32[8]{0:T(128)S(1)} %broadcast_multiply_fusion.5, f32[8,88,256]{2,1,0:T(8,128)} %fusion.18, f32[8,88,256]{2,1,0:T(8,128)} %fusion.17, f32[8,88,256]{2,1,0:T(8,128)} %fusion.24, ...), kind=kOutput, calls=%fused_computation.90 | convolution fusion | flops 188774400 | bytes 6807840 | tf_op jit(solution)/shard_map/hqk,qhe->khe/dot_general | solution.py:77
  183.2 2.9 %fusion.28 = bf16[8,88,256]{2,1,0:T(8,128)(2,1)S(1)} fusion(f32[8,88,256]{2,1,0:T(8,128)} %fusion.38, f32[8,88,256]{2,1,0:T(8,128)} %fusion.40, f32[8,88,256]{2,1,0:T(8,128)} %convolution_add_fusion.2, bf16[256,8,88]{0,2,1:T(8,128)(2,1)S(1)} %bitcast.177, f32[8,256,256]{2,1,0:T(8,128)} %fusion.76, f32[8,256]{1,0:T(8,128)S(1)} %compare_select_fusion.2, ...), kind=kOutput, calls=%fused_computation.50 | convolution fusion | flops 95092736 | bytes 4989216 | tf_op jit(solution)/shard_map/hqk,qhe->khe/dot_general | solution.py:80
  186.1 5.0 %fusion.71 = (f32[256]{0:T(256)S(1)}, f32[256]{0:T(256)S(1)}, f32[256,1408]{1,0:T(8,128)S(1)}) fusion(f32[256]{0:T(256)S(1)} %add_rsqrt_fusion.2, f32[256]{0:T(256)S(1)} %broadcast_multiply_fusion.4, bf16[256,1408]{1,0:T(8,128)(2,1)S(1)} %copy-done.2, f32[1408]{0:T(1024)S(1)} %copy-done.29, bf16[1408,2112]{0,1:T(8,128)(2,1)} %param.16, ...), kind=kOutput, calls=%fused_computation.158 | convolution fusion | flops 1528299008 | bytes 9201152 | tf_op jit(solution)/shard_map/dot_general | solution.py:200
  (151 shorter events, 56.1 us)
Async XLA Ops:
  2.5 4.9 %copy-start.29 = (f32[1408]{0:T(1024)S(1)}, f32[1408]{0:T(1024)}, u32[]{:S(2)}) copy-start(f32[1408]{0:T(1024)} %param.15) | copy-start | bytes 16900
  12.8 13.2 %copy-start.27 = (s32[4,4,2]{1,2,0:T(2,128)S(1)}, s32[4,4,2]{1,2,0:T(2,128)}, u32[]{:S(2)}) copy-start(s32[4,4,2]{1,2,0:T(2,128)} %param.14) | copy-start | bytes 388
  12.8 16.6 %copy-start.26 = (s32[4,4]{1,0:T(4,128)S(1)}, s32[4,4]{1,0:T(4,128)}, u32[]{:S(2)}) copy-start(s32[4,4]{1,0:T(4,128)} %param.13) | copy-start | bytes 196
  12.8 20.5 %copy-start.28 = (s32[1,1,256]{2,1,0:T(1,128)S(1)}, s32[1,1,256]{2,1,0:T(1,128)}, u32[]{:S(2)}) copy-start(s32[1,1,256]{2,1,0:T(1,128)} %param.12) | copy-start | bytes 3076
  13.9 29.0 %collective-permute-start = (bf16[1,1,256,2112]{2,3,1,0:T(8,128)(2,1)}, bf16[1,1,256,2112]{2,3,1,0:T(8,128)(2,1)}, u32[]{:S(2)}, u32[]{:S(2)}) collective-permute-start(bf16[1,1,256,2112]{2,3,1,0:T(8,128)(2,1)} %maximum_bitcast_fusion), channel_id=1, source_target_pairs={{0,4},{4,8},{8,12},{1,5},{5,9},{9,13},{2,6},{6,10},{10,14},{3,7},{... | collective-permute-start | bytes 3244040 | tf_op jit(solution)/shard_map/ppermute | solution.py:19
  17.4 31.8 %collective-permute-start.1 = (bf16[1,1,256,2112]{2,3,1,0:T(8,128)(2,1)}, bf16[1,1,256,2112]{2,3,1,0:T(8,128)(2,1)}, u32[]{:S(2)}, u32[]{:S(2)}) collective-permute-start(bf16[1,1,256,2112]{2,3,1,0:T(8,128)(2,1)} %maximum_bitcast_fusion), channel_id=1, source_target_pairs={{4,0},{8,4},{12,8},{5,1},{9,5},{13,9},{6,2},{10,6},{14,10},{7,3},{... | collective-permute-start | bytes 3244040 | tf_op jit(solution)/shard_map/ppermute | solution.py:22
  20.8 42.9 %all-to-all-start.1 = ((bf16[4,64,1408]{2,1,0:T(8,128)(2,1)}), bf16[4,64,1408]{2,1,0:T(8,128)(2,1)S(1)}, u32[]{:S(2)}, u32[]{:S(2)}) async-start(bf16[4,64,1408]{2,1,0:T(8,128)(2,1)} %bitcast.30), calls=%async_computation.1 | async-start | bytes 1441792 | tf_op jit(solution)/shard_map/all_to_all | solution.py:125
  33.4 23.2 %copy-start.30 = (f32[8]{0:T(128)S(1)}, f32[8]{0:T(128)}, u32[]{:S(2)}) copy-start(f32[8]{0:T(128)} %param.17) | copy-start | bytes 100
  53.2 57.7 %collective-permute-start.3 = (bf16[3,1,256,2112]{2,3,1,0:T(8,128)(2,1)}, bf16[3,1,256,2112]{2,3,1,0:T(8,128)(2,1)}, u32[]{:S(2)}, u32[]{:S(2)}) collective-permute-start(bf16[3,1,256,2112]{2,3,1,0:T(8,128)(2,1)} %pad_maximum_fusion), channel_id=1, source_target_pairs={{1,0},{2,1},{3,2},{5,4},{6,5},{7,6},{9,8},{10,9},{11,10},{13,12},{... | collective-permute-start | bytes 9732104 | tf_op jit(solution)/shard_map/ppermute | solution.py:22
  58.7 54.3 %collective-permute-start.2 = (bf16[3,1,256,2112]{2,3,1,0:T(8,128)(2,1)}, bf16[3,1,256,2112]{2,3,1,0:T(8,128)(2,1)}, u32[]{:S(2)}, u32[]{:S(2)}) collective-permute-start(bf16[3,1,256,2112]{2,3,1,0:T(8,128)(2,1)} %pad_maximum_fusion), channel_id=1, source_target_pairs={{0,1},{1,2},{2,3},{4,5},{5,6},{6,7},{8,9},{9,10},{10,11},{12,13},{... | collective-permute-start | bytes 9732104 | tf_op jit(solution)/shard_map/ppermute | solution.py:19
  68.4 11.6 %collective-permute-start.7 = (bf16[1,1,256,704]{2,3,1,0:T(8,128)(2,1)S(1)}, bf16[1,1,256,704]{2,3,1,0:T(8,128)(2,1)S(1)}, u32[]{:S(2)}, u32[]{:S(2)}) collective-permute-start(bf16[1,1,256,704]{2,3,1,0:T(8,128)(2,1)S(1)} %bitcast.165), channel_id=1, source_target_pairs={{4,0},{8,4},{12,8},{5,1},{9,5},{13,9},{6,2},{10,6},{14,10},{7,3},{... | collective-permute-start | bytes 1081352 | tf_op jit(solution)/shard_map/ppermute | solution.py:22
  71.8 11.3 %collective-permute-start.5 = (bf16[1,1,256,704]{2,3,1,0:T(8,128)(2,1)S(1)}, bf16[1,1,256,704]{2,3,1,0:T(8,128)(2,1)S(1)}, u32[]{:S(2)}, u32[]{:S(2)}) collective-permute-start(bf16[1,1,256,704]{2,3,1,0:T(8,128)(2,1)S(1)} %bitcast.166), channel_id=1, source_target_pairs={{0,4},{4,8},{8,12},{1,5},{5,9},{9,13},{2,6},{6,10},{10,14},{3,7},{... | collective-permute-start | bytes 1081352 | tf_op jit(solution)/shard_map/ppermute | solution.py:19
  75.8 7.4 %copy-start.12 = (bf16[256,704]{0,1:T(8,128)(2,1)}, bf16[256,704]{0,1:T(8,128)(2,1)S(1)}, u32[]{:S(2)}) copy-start(bf16[256,704]{0,1:T(8,128)(2,1)S(1)} %slice.132) | copy-start | bytes 1081348
  77.0 10.8 %copy-start.10 = (bf16[256,704]{0,1:T(8,128)(2,1)}, bf16[256,704]{0,1:T(8,128)(2,1)S(1)}, u32[]{:S(2)}) copy-start(bf16[256,704]{0,1:T(8,128)(2,1)S(1)} %slice.135) | copy-start | bytes 1081348
  78.8 10.8 %copy-start.4 = (bf16[1280,1408]{0,1:T(8,128)(2,1)S(1)}, bf16[1280,1408]{0,1:T(8,128)(2,1)}, u32[]{:S(2)}) copy-start(bf16[1280,1408]{0,1:T(8,128)(2,1)} %fusion.51) | copy-start | bytes 10813444
  80.0 9.6 %copy-start.21 = (bf16[1,1,256,704]{2,3,1,0:T(8,128)(2,1)}, bf16[1,1,256,704]{2,3,1,0:T(8,128)(2,1)S(1)}, u32[]{:S(2)}) copy-start(bf16[1,1,256,704]{2,3,1,0:T(8,128)(2,1)S(1)} %collective-permute-done.7) | copy-start | bytes 1081348
  83.1 6.5 %copy-start.23 = (bf16[1,1,256,704]{2,3,1,0:T(8,128)(2,1)}, bf16[1,1,256,704]{2,3,1,0:T(8,128)(2,1)S(1)}, u32[]{:S(2)}) copy-start(bf16[1,1,256,704]{2,3,1,0:T(8,128)(2,1)S(1)} %collective-permute-done.5) | copy-start | bytes 1081348
  83.2 19.5 %collective-permute-start.11 = (bf16[3,1,256,704]{2,3,1,0:T(8,128)(2,1)S(1)}, bf16[3,1,256,704]{2,3,1,0:T(8,128)(2,1)S(1)}, u32[]{:S(2)}, u32[]{:S(2)}) collective-permute-start(bf16[3,1,256,704]{2,3,1,0:T(8,128)(2,1)S(1)} %pad_maximum_fusion.1), channel_id=1, source_target_pairs={{1,0},{2,1},{3,2},{5,4},{6,5},{7,6},{9,8},{10,9},{11,10},{13,12},{... | collective-permute-start | bytes 3244040 | tf_op jit(solution)/shard_map/ppermute | solution.py:22
  85.1 25.0 %collective-permute-start.9 = (bf16[3,1,256,704]{2,3,1,0:T(8,128)(2,1)S(1)}, bf16[3,1,256,704]{2,3,1,0:T(8,128)(2,1)S(1)}, u32[]{:S(2)}, u32[]{:S(2)}) collective-permute-start(bf16[3,1,256,704]{2,3,1,0:T(8,128)(2,1)S(1)} %pad_maximum_fusion.1), channel_id=1, source_target_pairs={{0,1},{1,2},{2,3},{4,5},{5,6},{6,7},{8,9},{9,10},{10,11},{12,13},{... | collective-permute-start | bytes 3244040 | tf_op jit(solution)/shard_map/ppermute | solution.py:19
  123.1 34.4 %collective-permute-start.6 = (f32[1,1,2,8,256]{4,3,2,1,0:T(8,128)S(1)}, f32[1,1,2,8,256]{4,3,2,1,0:T(8,128)S(1)}, u32[]{:S(2)}, u32[]{:S(2)}) collective-permute-start(f32[1,1,2,8,256]{4,3,2,1,0:T(8,128)S(1)} %maximum_bitcast_fusion.1), channel_id=1, source_target_pairs={{4,0},{8,4},{12,8},{5,1},{9,5},{13,9},{6,2},{10,6},{14,10},{7,3},{... | collective-permute-start | bytes 49160 | tf_op jit(solution)/shard_map/ppermute | solution.py:22
  126.5 31.1 %collective-permute-start.4 = (f32[1,1,2,8,256]{4,3,2,1,0:T(8,128)S(1)}, f32[1,1,2,8,256]{4,3,2,1,0:T(8,128)S(1)}, u32[]{:S(2)}, u32[]{:S(2)}) collective-permute-start(f32[1,1,2,8,256]{4,3,2,1,0:T(8,128)S(1)} %maximum_bitcast_fusion.1), channel_id=1, source_target_pairs={{0,4},{4,8},{8,12},{1,5},{5,9},{9,13},{2,6},{6,10},{10,14},{3,7},{... | collective-permute-start | bytes 49160 | tf_op jit(solution)/shard_map/ppermute | solution.py:19
  144.2 8.8 %copy-start.14 = (bf16[256,704]{0,1:T(8,128)(2,1)S(1)}, bf16[256,704]{0,1:T(8,128)(2,1)}, u32[]{:S(2)}) copy-start(bf16[256,704]{0,1:T(8,128)(2,1)} %slice.142) | copy-start | bytes 1081348
  147.4 45.3 %all-to-all-start = ((bf16[4,64,1408]{2,1,0:T(8,128)(2,1)}), bf16[4,64,1408]{2,1,0:T(8,128)(2,1)}, u32[]{:S(2)}, u32[]{:S(2)}) async-start(bf16[4,64,1408]{2,1,0:T(8,128)(2,1)} %bitcast.151), calls=%async_computation | async-start | bytes 1441792 | tf_op jit(solution)/shard_map/all_to_all | solution.py:191
  154.8 7.3 %copy-start.7 = (f32[8,256,256]{2,1,0:T(8,128)S(1)}, f32[8,256,256]{2,1,0:T(8,128)}, u32[]{:S(2)}) copy-start(f32[8,256,256]{2,1,0:T(8,128)} %fusion.75) | copy-start | bytes 6291460
  154.8 7.3 %copy-start.17 = (f32[8,88,256]{2,1,0:T(8,128)S(1)}, f32[8,88,256]{2,1,0:T(8,128)}, u32[]{:S(2)}) copy-start(f32[8,88,256]{2,1,0:T(8,128)} %fusion.34) | copy-start | bytes 2162692
  154.8 7.3 %copy-start.24 = (bf16[1,1,256,704]{2,3,1,0:T(8,128)(2,1)S(1)}, bf16[1,1,256,704]{2,3,1,0:T(8,128)(2,1)}, u32[]{:S(2)}) copy-start(bf16[1,1,256,704]{2,3,1,0:T(8,128)(2,1)} %copy-done.23) | copy-start | bytes 1081348
  157.6 10.0 %collective-permute-start.10 = (f32[3,1,2,8,256]{4,3,2,1,0:T(8,128)S(1)}, f32[3,1,2,8,256]{4,3,2,1,0:T(8,128)S(1)}, u32[]{:S(2)}, u32[]{:S(2)}) collective-permute-start(f32[3,1,2,8,256]{4,3,2,1,0:T(8,128)S(1)} %pad_maximum_fusion.2), channel_id=1, source_target_pairs={{1,0},{2,1},{3,2},{5,4},{6,5},{7,6},{9,8},{10,9},{11,10},{13,12},{... | collective-permute-start | bytes 147464 | tf_op jit(solution)/shard_map/ppermute | solution.py:22
  159.5 15.0 %collective-permute-start.8 = (f32[3,1,2,8,256]{4,3,2,1,0:T(8,128)S(1)}, f32[3,1,2,8,256]{4,3,2,1,0:T(8,128)S(1)}, u32[]{:S(2)}, u32[]{:S(2)}) collective-permute-start(f32[3,1,2,8,256]{4,3,2,1,0:T(8,128)S(1)} %pad_maximum_fusion.2), channel_id=1, source_target_pairs={{0,1},{1,2},{2,3},{4,5},{5,6},{6,7},{8,9},{9,10},{10,11},{12,13},{... | collective-permute-start | bytes 147464 | tf_op jit(solution)/shard_map/ppermute | solution.py:19
  163.8 3.8 %copy-start.20 = (bf16[1,1,256,704]{2,3,1,0:T(8,128)(2,1)S(1)}, bf16[1,1,256,704]{2,3,1,0:T(8,128)(2,1)}, u32[]{:S(2)}) copy-start(bf16[1,1,256,704]{2,3,1,0:T(8,128)(2,1)} %slice.144) | copy-start | bytes 1081348
  179.6 3.6 %copy-start.22 = (bf16[1,1,256,704]{2,3,1,0:T(8,128)(2,1)S(1)}, bf16[1,1,256,704]{2,3,1,0:T(8,128)(2,1)}, u32[]{:S(2)}) copy-start(bf16[1,1,256,704]{2,3,1,0:T(8,128)(2,1)} %copy-done.21) | copy-start | bytes 1081348
  186.1 5.1 %copy-start.3 = (bf16[256,1408]{1,0:T(8,128)(2,1)S(1)}, bf16[256,1408]{1,0:T(8,128)(2,1)}, u32[]{:S(2)}) copy-start(bf16[256,1408]{1,0:T(8,128)(2,1)} %gather_fusion) | copy-start | bytes 2162692
  186.1 5.1 %copy-start.6 = (bf16[256,1408]{1,0:T(8,128)(2,1)S(1)}, bf16[256,1408]{1,0:T(8,128)(2,1)}, u32[]{:S(2)}) copy-start(bf16[256,1408]{1,0:T(8,128)(2,1)} %gather_fusion.1) | copy-start | bytes 2162692
  (13 other events, 32.1 us)
where the time goes:
time: 198 us; the launch traced here: 195 us
  matrix products  60.3 us (30%)
  starting transfers between devices  44.6 us (23%)
  waiting for transfers between devices  37.5 us (19%)
  local copies, waits for them, and re-layouts  24.7 us (12%)
  other arithmetic  23.7 us (12%)
  between operations  3.95 us (2%)
    ppermute x6, waiting for transfers between devices, extended_2(): lax.ppermute(lax.slice_in_dim(block, block.shape[dim] - width, None, axis...  19.2 us
    ppermute x6, waiting for transfers between devices, extended_2(): lax.ppermute(lax.slice_in_dim(block, 0, width, axis=dim), axis, backward)  18.3 us
    ppermute x6, starting transfers between devices, extended_2(): lax.ppermute(lax.slice_in_dim(block, block.shape[dim] - width, None, axis...  17.8 us
    ppermute x6, starting transfers between devices, extended_2(): lax.ppermute(lax.slice_in_dim(block, 0, width, axis=dim), axis, backward)  15.9 us
    dot_general x5, matrix products, key_back(): jnp.einsum('hqk,qhe->khe', score_grad, queries, preferred_element_type=jn...  15.4 us
    dot_general x5, matrix products, key_back(): jnp.einsum('hqk,qhe->khe', rounded, out_grad, preferred_element_type=jnp....  10.6 us
    unnamed x71, local copies, waits for them, and re-layouts  7.72 us
    dot_general x4, matrix products, per_device(): jnp.einsum('qhe,khe->hqk', far_queries, key_norm, preferred_element_type=...  7.17 us
  transfers between devices with their start and end apart: 14, of which 6 were waited for; matrix products, arithmetic and copies ran while one was open for 43% of the time, Pallas kernels for 0%

commit v1 on v0

v1 whole, which is shorter than its diff:
```python
import functools
import math

import jax
import jax.numpy as jnp
from jax import lax
from jax.experimental import pallas as pl
from jax.experimental.pallas import tpu as pltpu
from jax.sharding import PartitionSpec as P

MESH = pl.DeviceIdType.MESH
BF16 = jnp.bfloat16
F32 = jnp.float32
LANES = 128
NN = (((1,), (0,)), ((), ()))
NT = (((1,), (1,)), ((), ()))
TN = (((0,), (0,)), ((), ()))


def dot(a, b, dims):
    return lax.dot_general(a, b, dims, preferred_element_type=F32)


def tiles(total, step=256):
    return [(at, min(step, total - at)) for at in range(0, total, step)]


def kernel(
    sizes,
    patches_hbm, keep_ref, dest_ref, counts_ref, link_ref, gain_ref, wqkv_hbm, scale_ref, wout_hbm,
    cot_hbm,
    layer_hbm, grad_hbm,
    patches, wqkv, wout, incoming, kept, token, scaled, inv_std, normed, proj, raw, rms, qh, doh, kvh,
    kv_send, kv_far, exps, dps, att_t, own_dkv, far_dkv, dkv_send, dkv_far, pgh, pg, outgoing, grad_out,
    load_sem, cot_send_sem, cot_recv_sem, kv_send_sem, kv_recv_sem, dkv_send_sem, dkv_recv_sem,
    out_send_sem, out_recv_sem, own_sem,
):
    rows, cols, keep, depth, patch_count, heads, hd = sizes
    cap = keep // rows
    group = lax.axis_index("groups")
    row = lax.axis_index("row")
    col = lax.axis_index("col")

    loads = [
        pltpu.make_async_copy(patches_hbm, patches, load_sem.at[0]),
        pltpu.make_async_copy(wqkv_hbm, wqkv, load_sem.at[1]),
        pltpu.make_async_copy(wout_hbm, wout, load_sem.at[2]),
    ]
    for load in loads:
        load.start()

    near = [
        (row > 0, (group, row - 1, col)),
        (row < rows - 1, (group, row + 1, col)),
        (col > 0, (group, row, col - 1)),
        (col < cols - 1, (group, row, col + 1)),
    ]
    opposite = [1, 0, 3, 2]
    peers = [lax.rem(row + shift, rows) for shift in range(rows)]

    barrier = pltpu.get_barrier_semaphore()
    for shift in range(1, rows):
        pl.semaphore_signal(
            barrier, inc=1, device_id=(group, peers[shift], col), device_id_type=MESH
        )
    for exists, target in near[2:]:

        @pl.when(exists)
        def _():
            pl.semaphore_signal(barrier, inc=1, device_id=target, device_id_type=MESH)

    beside = jnp.where(col > 0, 1, 0) + jnp.where(col < cols - 1, 1, 0)
    pl.semaphore_wait(barrier, rows - 1 + beside)

    def block_of(index):
        return pl.ds(pl.multiple_of(index * cap, cap), cap)

    cot_copies = [
        pltpu.make_async_remote_copy(
            src_ref=cot_hbm.at[block_of(peers[shift])],
            dst_ref=incoming.at[block_of(row)],
            send_sem=cot_send_sem.at[shift],
            recv_sem=cot_recv_sem.at[shift],
            device_id=(group, peers[shift], col),
            device_id_type=MESH,
        )
        for shift in range(1, rows)
    ]
    for copy in cot_copies:
        copy.start()
    own_cot = pltpu.make_async_copy(
        cot_hbm.at[block_of(row)], incoming.at[block_of(row)], own_sem.at[0]
    )
    own_cot.start()

    for side, (exists, _) in enumerate(near):

        @pl.when(jnp.logical_not(exists))
        def _():
            kv_far[side] = jnp.zeros(kv_far.shape[1:], BF16)
            dkv_far[side] = jnp.zeros(dkv_far.shape[1:], BF16)

    pick = (
        lax.broadcasted_iota(jnp.int32, (patch_count, keep), 0) == keep_ref[...]
    ).astype(F32).astype(BF16)
    loads[0].wait()
    for at, size in tiles(depth):
        kept[:, at : at + size] = dot(pick, patches[:, at : at + size], TN).astype(BF16)

    values = kept[...].astype(F32)
    centred = values - jnp.mean(values, axis=-1, keepdims=True)
    inv = lax.rsqrt(jnp.mean(centred * centred, axis=-1, keepdims=True) + 1e-06)
    inv_std[...] = inv
    scaled[...] = centred * inv
    normed[...] = (scaled[...] * gain_ref[...]).astype(BF16)

    loads[1].wait()
    for at, size in tiles(3 * heads * hd):
        proj[:, at : at + size] = dot(normed[...], wqkv[:, at : at + size], NN)

    pieces = [None] * (2 * heads)
    for piece in range(3 * heads):
        part = proj[:, piece * hd : (piece + 1) * hd]
        if piece < 2 * heads:
            mean = jnp.sum(part * part, axis=-1, keepdims=True) * (1.0 / hd)
            inv = lax.rsqrt(mean + 1e-06)
            raw[piece, :, :hd] = part
            rms[piece] = inv
            part = (part * inv).astype(BF16)
        else:
            part = part.astype(BF16)
        if piece < heads:
            qh[piece] = jnp.zeros(qh.shape[1:], BF16)
            qh[piece, :, :hd] = part
        else:
            which, head = divmod(piece - heads, heads)
            pieces[2 * head + which] = part
            kvh[0, 2 * head + which] = jnp.zeros(kvh.shape[2:], BF16)
            kvh[0, 2 * head + which, :, :hd] = part
    kv_send[...] = jnp.concatenate(pieces, axis=1)

    kv_copies = []
    for side, (exists, target) in enumerate(near):
        copy = pltpu.make_async_remote_copy(
            src_ref=kv_send,
            dst_ref=kv_far.at[opposite[side]],
            send_sem=kv_send_sem.at[side],
            recv_sem=kv_recv_sem.at[opposite[side]],
            device_id=target,
            device_id_type=MESH,
        )
        kv_copies.append(copy)

        @pl.when(exists)
        def _():
            copy.start()

    slot_pick = (
        lax.broadcasted_iota(jnp.int32, (keep, keep), 0) == dest_ref[...]
    ).astype(F32).astype(BF16)
    for copy in cot_copies:
        copy.wait()
    own_cot.wait()
    for at, size in tiles(depth):
        token[:, at : at + size] = dot(slot_pick, incoming[:, at : at + size], TN).astype(BF16)
    loads[2].wait()
    out_grad = dot(token[...], wout[...], NT).astype(BF16)
    for head in range(heads):
        doh[head] = jnp.zeros(doh.shape[1:], BF16)
        doh[head, :, :hd] = out_grad[:, head * hd : (head + 1) * hd]

    above_row = jnp.maximum(row - 1, 0)
    below_row = jnp.minimum(row + 1, rows - 1)
    left_col = jnp.maximum(col - 1, 0)
    right_col = jnp.minimum(col + 1, cols - 1)
    limits = [
        counts_ref[row, col],
        jnp.where(row > 0, counts_ref[above_row, col] * link_ref[above_row, col, 1], 0),
        jnp.where(row < rows - 1, counts_ref[below_row, col] * link_ref[row, col, 1], 0),
        jnp.where(col > 0, counts_ref[row, left_col] * link_ref[row, left_col, 0], 0),
        jnp.where(col < cols - 1, counts_ref[row, right_col] * link_ref[row, col, 0], 0),
    ]

    for side, (exists, _) in enumerate(near):

        @pl.when(exists)
        def _():
            kv_copies[side].wait_send()
            pltpu.make_async_remote_copy(
                src_ref=kv_send,
                dst_ref=kv_far.at[side],
                send_sem=kv_send_sem.at[side],
                recv_sem=kv_recv_sem.at[side],
                device_id=near[side][1],
                device_id_type=MESH,
            ).wait_recv()

        far = kv_far[side]
        for piece in range(2 * heads):
            kvh[1 + side, piece] = jnp.zeros(kvh.shape[2:], BF16)
            kvh[1 + side, piece, :, :hd] = far[:, piece * hd : (piece + 1) * hd]

    panels = 5
    key_at = lax.broadcasted_iota(jnp.int32, (keep, keep), 0)

    def head_step(head, carry):
        coef = scale_ref[head] * (1.0 / math.sqrt(hd))
        query = qh[head]
        grad = doh[head]
        total = jnp.zeros((1, keep), F32)
        for panel in range(panels):
            scores = dot(kvh[panel, 2 * head], query, NT) * coef
            raised = jnp.where(key_at < limits[panel], jnp.exp(scores), 0.0)
            total = total + jnp.sum(raised, axis=0, keepdims=True)
            exps[panel] = raised
        inverse = 1.0 / total
        delta = jnp.zeros((1, keep), F32)
        attended = jnp.zeros((LANES, keep), F32)
        for panel in range(panels):
            value = kvh[panel, 2 * head + 1]
            weights = exps[panel] * inverse
            exps[panel] = weights
            rounded = weights.astype(BF16)
            attended = attended + dot(value, rounded, TN)
            dot_grad = dot(value, grad, NT)
            dps[panel] = dot_grad
            delta = delta + jnp.sum(weights * dot_grad, axis=0, keepdims=True)
            value_grad = dot(rounded, grad, NN)
            if panel == 0:
                own_dkv[2 * head + 1] = value_grad
            else:
                far_dkv[panel - 1, 2 * head + 1] = value_grad.astype(BF16)
        att_t[pl.ds(pl.multiple_of(head * hd, 8), hd), :] = attended[:hd]
        query_grad = jnp.zeros((LANES, keep), F32)
        for panel in range(panels):
            score_grad = (exps[panel] * (dps[panel] - delta)).astype(BF16)
            query_grad = query_grad + dot(kvh[panel, 2 * head], score_grad, TN)
            key_grad = dot(score_grad, query, NN) * coef
            if panel == 0:
                own_dkv[2 * head] = key_grad
            else:
                far_dkv[panel - 1, 2 * head] = key_grad.astype(BF16)
        upstream = query_grad.T[:, :hd] * coef
        split = raw[head, :, :hd]
        inv = rms[head]
        inner = jnp.sum(upstream * split, axis=-1, keepdims=True) * (1.0 / hd)
        pgh[head, :, :hd] = (inv * (upstream - split * (inv * inv * inner))).astype(BF16)
        return carry

    lax.fori_loop(0, heads, head_step, 0)

    dkv_copies = []
    for side, (exists, target) in enumerate(near):
        dkv_send[side] = jnp.concatenate(
            [far_dkv[side, piece, :, :hd] for piece in range(2 * heads)], axis=1
        )
        copy = pltpu.make_async_remote_copy(
            src_ref=dkv_send.at[side],
            dst_ref=dkv_far.at[opposite[side]],
            send_sem=dkv_send_sem.at[side],
            recv_sem=dkv_recv_sem.at[opposite[side]],
            device_id=target,
            device_id_type=MESH,
        )
        dkv_copies.append(copy)

        @pl.when(exists)
        def _():
            copy.start()

    attended = att_t[...].astype(BF16)
    for at, size in tiles(depth):
        span = slice(at, at + size)
        kept_out = (kept[:, span].astype(F32) + dot(attended, wout[:, span], TN)).astype(BF16)
        outgoing[:, span] = dot(slot_pick, kept_out, NN).astype(BF16)
    out_copies = [
        pltpu.make_async_remote_copy(
            src_ref=outgoing.at[block_of(peers[shift])],
            dst_ref=layer_hbm.at[block_of(row)],
            send_sem=out_send_sem.at[shift],
            recv_sem=out_recv_sem.at[shift],
            device_id=(group, peers[shift], col),
            device_id_type=MESH,
        )
        for shift in range(1, rows)
    ]
    for copy in out_copies:
        copy.start()
    own_out = pltpu.make_async_copy(
        outgoing.at[block_of(row)], layer_hbm.at[block_of(row)], own_sem.at[1]
    )
    own_out.start()

    for side, (exists, target) in enumerate(near):

        @pl.when(exists)
        def _():
            dkv_copies[side].wait_send()
            pltpu.make_async_remote_copy(
                src_ref=dkv_send.at[side],
                dst_ref=dkv_far.at[side],
                send_sem=dkv_send_sem.at[side],
                recv_sem=dkv_recv_sem.at[side],
                device_id=target,
                device_id_type=MESH,
            ).wait_recv()

    for head in range(heads):
        for which in range(2):
            piece = 2 * head + which
            span = slice(piece * hd, (piece + 1) * hd)
            upstream = own_dkv[piece, :, :hd]
            for side in range(4):
                upstream = upstream + dkv_far[side, :, span].astype(F32)
            if which == 0:
                split = raw[heads + head, :, :hd]
                inv = rms[heads + head]
                inner = jnp.sum(upstream * split, axis=-1, keepdims=True) * (1.0 / hd)
                upstream = inv * (upstream - split * (inv * inv * inner))
            pgh[heads * (1 + which) + head, :, :hd] = upstream.astype(BF16)
    pg[...] = jnp.concatenate([pgh[piece, :, :hd] for piece in range(3 * heads)], axis=1)

    gained = proj
    for at, size in tiles(depth):
        span = slice(at, at + size)
        gained[:, span] = dot(pg[...], wqkv[span, :], NT) * gain_ref[:, span]
    grads = gained[:, :depth]
    mean_grad = jnp.mean(grads, axis=-1, keepdims=True)
    mean_scaled = jnp.mean(grads * scaled[...], axis=-1, keepdims=True)
    grad_out[...] = (
        token[...].astype(F32) + inv_std[...] * (grads - mean_grad - scaled[...] * mean_scaled)
    ).astype(BF16)
    store = pltpu.make_async_copy(grad_out, grad_hbm, own_sem.at[2])
    store.start()
    for copy in out_copies:
        copy.wait()
    own_out.wait()
    store.wait()


def per_device(
    rows, cols,
    patches, keep_list, destination, counts, link_open, ln_gain, w_qkv, head_scale, w_out, cotangent,
):
    keep = keep_list.shape[2]
    patch_count, depth = patches.shape[2:]
    heads = head_scale.shape[0]
    width = w_out.shape[0]
    hd = width // heads
    sizes = (rows, cols, keep, depth, patch_count, heads, hd)
    hbm = pl.BlockSpec(memory_space=pl.ANY)
    vmem = pl.BlockSpec(memory_space=pltpu.VMEM)
    smem = pl.BlockSpec(memory_space=pltpu.SMEM)
    dma = pltpu.SemaphoreType.DMA
    scratch = [
        pltpu.VMEM((patch_count, depth), BF16),
        pltpu.VMEM((depth, 3 * width), BF16),
        pltpu.VMEM((width, depth), BF16),
        pltpu.VMEM((keep, depth), BF16),
        pltpu.VMEM((keep, depth), BF16),
        pltpu.VMEM((keep, depth), BF16),
        pltpu.VMEM((keep, depth), F32),
        pltpu.VMEM((keep, 1), F32),
        pltpu.VMEM((keep, depth), BF16),
        pltpu.VMEM((keep, 3 * width), F32),
        pltpu.VMEM((2 * heads, keep, LANES), F32),
        pltpu.VMEM((2 * heads, keep, 1), F32),
        pltpu.VMEM((heads, keep, LANES), BF16),
        pltpu.VMEM((heads, keep, LANES), BF16),
        pltpu.VMEM((5, 2 * heads, keep, LANES), BF16),
        pltpu.VMEM((keep, 2 * width), BF16),
        pltpu.VMEM((4, keep, 2 * width), BF16),
        pltpu.VMEM((5, keep, keep), F32),
        pltpu.VMEM((5, keep, keep), F32),
        pltpu.VMEM((width, keep), F32),
        pltpu.VMEM((2 * heads, keep, LANES), F32),
        pltpu.VMEM((4, 2 * heads, keep, LANES), BF16),
        pltpu.VMEM((4, keep, 2 * width), BF16),
        pltpu.VMEM((4, keep, 2 * width), BF16),
        pltpu.VMEM((3 * heads, keep, LANES), BF16),
        pltpu.VMEM((keep, 3 * width), BF16),
        pltpu.VMEM((keep, depth), BF16),
        pltpu.VMEM((keep, depth), BF16),
        dma((3,)),
        dma((rows,)),
        dma((rows,)),
        dma((4,)),
        dma((4,)),
        dma((4,)),
        dma((4,)),
        dma((rows,)),
        dma((rows,)),
        dma((3,)),
    ]
    layer_out, patch_grad = pl.pallas_call(
        functools.partial(kernel, sizes),
        out_shape=(
            jax.ShapeDtypeStruct((keep, depth), BF16),
            jax.ShapeDtypeStruct((keep, depth), BF16),
        ),
        in_specs=[hbm, vmem, vmem, smem, smem, vmem, hbm, smem, hbm, hbm],
        out_specs=(hbm, hbm),
        scratch_shapes=scratch,
        compiler_params=pltpu.CompilerParams(
            collective_id=0, has_side_effects=True, vmem_limit_bytes=60 * 2**20
        ),
    )(
        patches[0, 0], keep_list[0], destination[0], counts, link_open, ln_gain[None], w_qkv,
        head_scale, w_out, cotangent[0, 0],
    )
    return (layer_out[None, None], patch_grad[None, None])


def solution(mesh):
    window = P(("groups", "row"), "col", None, None)
    slots = P(("groups", "row"), "col", None)
    placed = (
        window, slots, slots, P("groups", None), P("groups", None, None), P(), P(), P(), P(), window,
    )
    return jax.shard_map(
        functools.partial(per_device, mesh.shape["row"], mesh.shape["col"]),
        mesh=mesh,
        in_specs=placed,
        out_specs=(window, window),
        check_vma=False,
    )
```

time: 198 us -> 106 us (0.54); the launches traced: 195 us -> 106 us
  Pallas kernels: 0 us -> 89.3 us
  matrix products: 60.3 us -> 0 us
  starting transfers between devices: 44.6 us -> 0 us
  waiting for transfers between devices: 37.5 us -> 0 us
  other arithmetic: 23.7 us -> 0 us
  local copies, waits for them, and re-layouts: 24.7 us -> 15.6 us
  between operations: 3.95 us -> 0.64 us
    pallas_call x0 -> x1, Pallas kernels: none -> 89.3 us  [per_device(): pl.pallas_call(functools.partial(kernel, sizes), out_shape=(jax.ShapeDtyp...]
    dot_general x22 -> x0, matrix products: 60.3 us -> none  [the longest x5 15.4 us: key_back(): jnp.einsum('hqk,qhe->khe', score_grad, queries, preferred_element_type=jn...]
    ppermute x12 -> x0, waiting for transfers between devices: 37.5 us -> none  [the longest x6 19.2 us: extended_2(): lax.ppermute(lax.slice_in_dim(block, block.shape[dim] - width, None, axis...]
    ppermute x12 -> x0, starting transfers between devices: 33.7 us -> none  [the longest x6 17.8 us: extended_2(): lax.ppermute(lax.slice_in_dim(block, block.shape[dim] - width, None, axis...]
    all_to_all x2 -> x0, starting transfers between devices: 10.9 us -> none  [the longest x1 5.61 us: per_device(): lax.all_to_all(outgoing.reshape(row_total, slot_cap, D), 'row', split_axi...]
    unnamed x71 -> x4, local copies, waits for them, and re-layouts: 7.72 us -> 14.3 us
    convert_element_type x3 -> x0, other arithmetic: 6.37 us -> none  [the longest x1 6.12 us: score_back(): return ((weights * (dot_grad - row_delta)).astype(jnp.bfloat16), row_delta)]
    slice x9 -> x0, local copies, waits for them, and re-layouts: 5.59 us -> none  [the longest x4 3.69 us: per_device(): far_queries = extended[grid_row, grid_col][:, :width].reshape(head_shape)]
  transfers between devices with their start and end apart: 14 -> 0, of which waited for: 6 -> 0; matrix products, arithmetic and copies ran while one was open for 43% -> 0% of each run, Pallas kernels for 0% -> 0%
where the time goes in v1:
time: 106 us
  Pallas kernels  89.3 us (84%)
  local copies, waits for them, and re-layouts  15.6 us (15%)
    pallas_call x1, Pallas kernels, per_device(): pl.pallas_call(functools.partial(kernel, sizes), out_shape=(jax.ShapeDtyp...  89.3 us
    unnamed x4, local copies, waits for them, and re-layouts  14.3 us

profile of v1, /device:TPU:14, one launch (start us, length us, event | category | flops | bytes accessed | tf_op | source)
XLA Modules:
  0.0 105.6 jit_solution(15603317961256512747)
XLA Ops:
  0.6 1.3 %broadcast_in_dim.9.gain_ref = f32[1,1408]{1,0:T(1,128)} reshape(f32[1408]{0:T(1024)} %param.15) | data formatting | bytes 11264 | tf_op jit(solution)/shard_map/broadcast_in_dim | solution.py:408
  1.9 1.4 %copy.12.link_ref = s32[4,4,2]{2,1,0:T(4,128)} copy(s32[4,4,2]{1,2,0:T(2,128)} %param.14) | data formatting | bytes 256 | tf_op args[4]
  3.3 8.9 %copy.13.wqkv_hbm = bf16[1408,2112]{1,0:T(8,128)(2,1)} copy(bf16[1408,2112]{0,1:T(8,128)(2,1)} %param.16) | data formatting | bytes 11894784 | tf_op args[6]
  12.2 89.3 %shard_map.113 = (bf16[256,1408]{1,0:T(8,128)(2,1)}, bf16[256,1408]{1,0:T(8,128)(2,1)}) custom-call(bf16[1024,1408]{1,0:T(8,128)(2,1)} %bitcast.6, s32[1,256]{1,0:T(1,128)} %bitcast.10, s32[1,256]{1,0:T(1,128)} %bitcast.11, s32[4,4]{1,0:T(4,128)} %counts_ref.1, s32[4,4,2]{2,1,0:T(4,128)} %copy.12.link_ref, f32[1,1408]{1,0:T(1,128)} %broadcast_in_dim.9.gain_ref, ...), custom_call_target="tpu_custom_call" | custom-call | tf_op jit(solution)/shard_map/pallas_call | solution.py:395
  101.5 2.0 %copy.16 = bf16[1,1,256,1408]{3,2,1,0:T(8,128)(2,1)} copy(bf16[1,1,256,1408]{3,2,1,0:T(8,128)(2,1)} %bitcast.8) | data formatting | bytes 1441792
  103.5 2.0 %copy.17 = bf16[1,1,256,1408]{3,2,1,0:T(8,128)(2,1)} copy(bf16[1,1,256,1408]{3,2,1,0:T(8,128)(2,1)} %bitcast.7) | data formatting | bytes 1441792

commit v2 on v1

--- a/solution.py
+++ b/solution.py
@@ -19,6 +19,19 @@
 
 def dot(a, b, dims):
     return lax.dot_general(a, b, dims, preferred_element_type=F32)
+
+
+PARTS = 2
+
+
+def cuts(heads, hd, up):
+    ends = [0]
+    for part in range(1, PARTS + 1):
+        columns = 2 * hd * (heads * part // PARTS)
+        if part < PARTS:
+            columns = (columns + (LANES - 1 if up else 0)) // LANES * LANES
+        ends.append(columns)
+    return list(zip(ends[:-1], ends[1:]))
 
 
 def tiles(total, step=256):
@@ -112,11 +125,11 @@
     inv = lax.rsqrt(jnp.mean(centred * centred, axis=-1, keepdims=True) + 1e-06)
     inv_std[...] = inv
     scaled[...] = centred * inv
-    normed[...] = (scaled[...] * gain_ref[...]).astype(BF16)
+    normed[...] = (scaled[...] * gain_ref[...][None, :]).astype(BF16)
 
     loads[1].wait()
     for at, size in tiles(3 * heads * hd):
-        proj[:, at : at + size] = dot(normed[...], wqkv[:, at : at + size], NN)
+        proj[:, at : at + size] = dot(normed[...], wqkv[at : at + size, :], NT)
 
     pieces = [None] * (2 * heads)
     for piece in range(3 * heads):
@@ -139,21 +152,34 @@
             kvh[0, 2 * head + which, :, :hd] = part
     kv_send[...] = jnp.concatenate(pieces, axis=1)
 
-    kv_copies = []
-    for side, (exists, target) in enumerate(near):
-        copy = pltpu.make_async_remote_copy(
-            src_ref=kv_send,
-            dst_ref=kv_far.at[opposite[side]],
-            send_sem=kv_send_sem.at[side],
-            recv_sem=kv_recv_sem.at[opposite[side]],
-            device_id=target,
+    def side_copy(part, source, target_buffer, send_sems, recv_sems, bounds, side, slot):
+        low, high = bounds[part]
+        return pltpu.make_async_remote_copy(
+            src_ref=source.at[:, low:high],
+            dst_ref=target_buffer.at[slot, :, low:high],
+            send_sem=send_sems.at[part, side],
+            recv_sem=recv_sems.at[part, slot],
+            device_id=near[side][1],
             device_id_type=MESH,
         )
-        kv_copies.append(copy)
-
-        @pl.when(exists)
-        def _():
-            copy.start()
+
+    kv_cuts = cuts(heads, hd, True)
+    dkv_cuts = cuts(heads, hd, False)
+
+    def kv_copy(part, side, slot):
+        return side_copy(part, kv_send, kv_far, kv_send_sem, kv_recv_sem, kv_cuts, side, slot)
+
+    def dkv_copy(part, side, slot):
+        return side_copy(
+            part, dkv_send.at[side], dkv_far, dkv_send_sem, dkv_recv_sem, dkv_cuts, side, slot
+        )
+
+    for part in range(PARTS):
+        for side, (exists, _) in enumerate(near):
+
+            @pl.when(exists)
+            def _():
+                kv_copy(part, side, opposite[side]).start()
 
     slot_pick = (
         lax.broadcasted_iota(jnp.int32, (keep, keep), 0) == dest_ref[...]
@@ -175,30 +201,11 @@
     right_col = jnp.minimum(col + 1, cols - 1)
     limits = [
         counts_ref[row, col],
-        jnp.where(row > 0, counts_ref[above_row, col] * link_ref[above_row, col, 1], 0),
-        jnp.where(row < rows - 1, counts_ref[below_row, col] * link_ref[row, col, 1], 0),
-        jnp.where(col > 0, counts_ref[row, left_col] * link_ref[row, left_col, 0], 0),
-        jnp.where(col < cols - 1, counts_ref[row, right_col] * link_ref[row, col, 0], 0),
-    ]
-
-    for side, (exists, _) in enumerate(near):
-
-        @pl.when(exists)
-        def _():
-            kv_copies[side].wait_send()
-            pltpu.make_async_remote_copy(
-                src_ref=kv_send,
-                dst_ref=kv_far.at[side],
-                send_sem=kv_send_sem.at[side],
-                recv_sem=kv_recv_sem.at[side],
-                device_id=near[side][1],
-                device_id_type=MESH,
-            ).wait_recv()
-
-        far = kv_far[side]
-        for piece in range(2 * heads):
-            kvh[1 + side, piece] = jnp.zeros(kvh.shape[2:], BF16)
-            kvh[1 + side, piece, :, :hd] = far[:, piece * hd : (piece + 1) * hd]
+        jnp.where(row > 0, counts_ref[above_row, col] * link_ref[above_row, 1, col], 0),
+        jnp.where(row < rows - 1, counts_ref[below_row, col] * link_ref[row, 1, col], 0),
+        jnp.where(col > 0, counts_ref[row, left_col] * link_ref[row, 0, left_col], 0),
+        jnp.where(col < cols - 1, counts_ref[row, right_col] * link_ref[row, 0, col], 0),
+    ]
 
     panels = 5
     key_at = lax.broadcasted_iota(jnp.int32, (keep, keep), 0)
@@ -247,26 +254,33 @@
         pgh[head, :, :hd] = (inv * (upstream - split * (inv * inv * inner))).astype(BF16)
         return carry
 
-    lax.fori_loop(0, heads, head_step, 0)
-
-    dkv_copies = []
-    for side, (exists, target) in enumerate(near):
-        dkv_send[side] = jnp.concatenate(
-            [far_dkv[side, piece, :, :hd] for piece in range(2 * heads)], axis=1
-        )
-        copy = pltpu.make_async_remote_copy(
-            src_ref=dkv_send.at[side],
-            dst_ref=dkv_far.at[opposite[side]],
-            send_sem=dkv_send_sem.at[side],
-            recv_sem=dkv_recv_sem.at[opposite[side]],
-            device_id=target,
-            device_id_type=MESH,
-        )
-        dkv_copies.append(copy)
-
-        @pl.when(exists)
-        def _():
-            copy.start()
+    for part in range(PARTS):
+        first, last = heads * part // PARTS, heads * (part + 1) // PARTS
+        for side, (exists, _) in enumerate(near):
+
+            @pl.when(exists)
+            def _():
+                kv_copy(part, side, side).wait_recv()
+
+            for piece in range(2 * first, 2 * last):
+                kvh[1 + side, piece] = jnp.zeros(kvh.shape[2:], BF16)
+                kvh[1 + side, piece, :, :hd] = kv_far[side, :, piece * hd : (piece + 1) * hd]
+        lax.fori_loop(first, last, head_step, 0)
+        low, high = dkv_cuts[part]
+        for side, (exists, _) in enumerate(near):
+            dkv_send[side, :, low:high] = jnp.concatenate(
+                [
+                    far_dkv[
+                        side, piece, :, max(low - piece * hd, 0) : min(high - piece * hd, hd)
+                    ]
+                    for piece in range(low // hd, -(-high // hd))
+                ],
+                axis=1,
+            )
+
+            @pl.when(exists)
+            def _():
+                dkv_copy(part, side, opposite[side]).start()
 
     attended = att_t[...].astype(BF16)
     for at, size in tiles(depth):
@@ -291,39 +305,40 @@
     )
     own_out.start()
 
-    for side, (exists, target) in enumerate(near):
-
-        @pl.when(exists)
-        def _():
-            dkv_copies[side].wait_send()
-            pltpu.make_async_remote_copy(
-                src_ref=dkv_send.at[side],
-                dst_ref=dkv_far.at[side],
-                send_sem=dkv_send_sem.at[side],
-                recv_sem=dkv_recv_sem.at[side],
-                device_id=target,
-                device_id_type=MESH,
-            ).wait_recv()
-
-    for head in range(heads):
-        for which in range(2):
-            piece = 2 * head + which
-            span = slice(piece * hd, (piece + 1) * hd)
-            upstream = own_dkv[piece, :, :hd]
-            for side in range(4):
-                upstream = upstream + dkv_far[side, :, span].astype(F32)
+    far_sum = proj
+    done = 0
+    for part in range(PARTS):
+        for side, (exists, _) in enumerate(near):
+
+            @pl.when(exists)
+            def _():
+                dkv_copy(part, side, side).wait_recv()
+
+        low, high = dkv_cuts[part]
+        for at, size in tiles(high - low):
+            span = slice(low + at, low + at + size)
+            far_sum[:, span] = (
+                dkv_far[0, :, span].astype(F32)
+                + dkv_far[1, :, span].astype(F32)
+                + dkv_far[2, :, span].astype(F32)
+                + dkv_far[3, :, span].astype(F32)
+            )
+        for piece in range(done, high // hd):
+            head, which = divmod(piece, 2)
+            upstream = own_dkv[piece, :, :hd] + far_sum[:, piece * hd : (piece + 1) * hd]
             if which == 0:
                 split = raw[heads + head, :, :hd]
                 inv = rms[heads + head]
                 inner = jnp.sum(upstream * split, axis=-1, keepdims=True) * (1.0 / hd)
                 upstream = inv * (upstream - split * (inv * inv * inner))
             pgh[heads * (1 + which) + head, :, :hd] = upstream.astype(BF16)
+        done = high // hd
     pg[...] = jnp.concatenate([pgh[piece, :, :hd] for piece in range(3 * heads)], axis=1)
 
     gained = proj
     for at, size in tiles(depth):
         span = slice(at, at + size)
-        gained[:, span] = dot(pg[...], wqkv[span, :], NT) * gain_ref[:, span]
+        gained[:, span] = dot(pg[...], wqkv[:, span], NN) * gain_ref[span][None, :]
     grads = gained[:, :depth]
     mean_grad = jnp.mean(grads, axis=-1, keepdims=True)
     mean_scaled = jnp.mean(grads * scaled[...], axis=-1, keepdims=True)
@@ -332,6 +347,14 @@
     ).astype(BF16)
     store = pltpu.make_async_copy(grad_out, grad_hbm, own_sem.at[2])
     store.start()
+    for part in range(PARTS):
+        for side, (exists, _) in enumerate(near):
+
+            @pl.when(exists)
+            def _():
+                kv_copy(part, side, side).wait_send()
+                dkv_copy(part, side, side).wait_send()
+
     for copy in out_copies:
         copy.wait()
     own_out.wait()
@@ -354,7 +377,7 @@
     dma = pltpu.SemaphoreType.DMA
     scratch = [
         pltpu.VMEM((patch_count, depth), BF16),
-        pltpu.VMEM((depth, 3 * width), BF16),
+        pltpu.VMEM((3 * width, depth), BF16),
         pltpu.VMEM((width, depth), BF16),
         pltpu.VMEM((keep, depth), BF16),
         pltpu.VMEM((keep, depth), BF16),
@@ -384,10 +407,10 @@
         dma((3,)),
         dma((rows,)),
         dma((rows,)),
-        dma((4,)),
-        dma((4,)),
-        dma((4,)),
-        dma((4,)),
+        dma((PARTS, 4)),
+        dma((PARTS, 4)),
+        dma((PARTS, 4)),
+        dma((PARTS, 4)),
         dma((rows,)),
         dma((rows,)),
         dma((3,)),
@@ -405,7 +428,7 @@
             collective_id=0, has_side_effects=True, vmem_limit_bytes=60 * 2**20
         ),
     )(
-        patches[0, 0], keep_list[0], destination[0], counts, link_open, ln_gain[None], w_qkv,
+        patches[0, 0], keep_list[0], destination[0], counts, link_open.transpose(0, 2, 1), ln_gain, w_qkv.T,
         head_scale, w_out, cotangent[0, 0],
     )
     return (layer_out[None, None], patch_grad[None, None])

time: 106 us -> 78.1 us (0.74)
  Pallas kernels: 89.3 us -> 73.2 us
  local copies, waits for them, and re-layouts: 15.6 us -> 4.04 us
    pallas_call x1, Pallas kernels: 89.3 us -> 73.2 us  [per_device(): pl.pallas_call(functools.partial(kernel, sizes), out_shape=(jax.ShapeDtyp...]
    unnamed x4 -> x2, local copies, waits for them, and re-layouts: 14.3 us -> 4.04 us
    broadcast_in_dim x1 -> x0, local copies, waits for them, and re-layouts: 1.29 us -> none  [per_device(): ln_gain[None]]
where the time goes in v2:
time: 78.1 us; the launch traced here: 77.9 us
  Pallas kernels  73.2 us (94%)
  local copies, waits for them, and re-layouts  4.04 us (5%)
    pallas_call x1, Pallas kernels, per_device(): pl.pallas_call(functools.partial(kernel, sizes), out_shape=(jax.ShapeDtyp...  73.2 us
    unnamed x2, local copies, waits for them, and re-layouts  4.04 us

profile of v2, /device:TPU:14, one launch (start us, length us, event | category | flops | bytes accessed | tf_op | source)
XLA Modules:
  0.0 77.9 jit_solution(16868906278595052075)
XLA Ops:
  0.6 73.2 %shard_map.113 = (bf16[256,1408]{1,0:T(8,128)(2,1)}, bf16[256,1408]{1,0:T(8,128)(2,1)}) custom-call(bf16[1024,1408]{1,0:T(8,128)(2,1)} %bitcast.9, s32[1,256]{1,0:T(1,128)} %bitcast.14, s32[1,256]{1,0:T(1,128)} %bitcast.15, s32[4,4]{1,0:T(4,128)} %counts_ref.1, s32[4,2,4]{2,1,0:T(2,128)} %bitcast.13, f32[1408]{0:T(1024)} %gain_ref.1, ...), custom_call_target="tpu_custom_call" | custom-call | tf_op jit(solution)/shard_map/pallas_call | solution.py:418
  73.8 2.0 %copy.14 = bf16[1,1,256,1408]{3,2,1,0:T(8,128)(2,1)} copy(bf16[1,1,256,1408]{3,2,1,0:T(8,128)(2,1)} %bitcast.11) | data formatting | bytes 1441792
  75.8 2.0 %copy.15 = bf16[1,1,256,1408]{3,2,1,0:T(8,128)(2,1)} copy(bf16[1,1,256,1408]{3,2,1,0:T(8,128)(2,1)} %bitcast.10) | data formatting | bytes 1441792

commit v3 on v2

--- a/solution.py
+++ b/solution.py
@@ -21,7 +21,7 @@
     return lax.dot_general(a, b, dims, preferred_element_type=F32)
 
 
-PARTS = 2
+PARTS = 4
 
 
 def cuts(heads, hd, up):
@@ -128,11 +128,13 @@
     normed[...] = (scaled[...] * gain_ref[...][None, :]).astype(BF16)
 
     loads[1].wait()
-    for at, size in tiles(3 * heads * hd):
-        proj[:, at : at + size] = dot(normed[...], wqkv[at : at + size, :], NT)
+    first_lane = heads * hd // LANES * LANES
+    for at, size in tiles(3 * heads * hd - first_lane):
+        span = slice(first_lane + at, first_lane + at + size)
+        proj[:, span] = dot(normed[...], wqkv[span, :], NT)
 
     pieces = [None] * (2 * heads)
-    for piece in range(3 * heads):
+    for piece in range(heads, 3 * heads):
         part = proj[:, piece * hd : (piece + 1) * hd]
         if piece < 2 * heads:
             mean = jnp.sum(part * part, axis=-1, keepdims=True) * (1.0 / hd)
@@ -142,14 +144,10 @@
             part = (part * inv).astype(BF16)
         else:
             part = part.astype(BF16)
-        if piece < heads:
-            qh[piece] = jnp.zeros(qh.shape[1:], BF16)
-            qh[piece, :, :hd] = part
-        else:
-            which, head = divmod(piece - heads, heads)
-            pieces[2 * head + which] = part
-            kvh[0, 2 * head + which] = jnp.zeros(kvh.shape[2:], BF16)
-            kvh[0, 2 * head + which, :, :hd] = part
+        which, head = divmod(piece - heads, heads)
+        pieces[2 * head + which] = part
+        kvh[0, 2 * head + which] = jnp.zeros(kvh.shape[2:], BF16)
+        kvh[0, 2 * head + which, :, :hd] = part
     kv_send[...] = jnp.concatenate(pieces, axis=1)
 
     def side_copy(part, source, target_buffer, send_sems, recv_sems, bounds, side, slot):
@@ -180,6 +178,16 @@
             @pl.when(exists)
             def _():
                 kv_copy(part, side, opposite[side]).start()
+
+    for at, size in tiles(first_lane):
+        proj[:, at : at + size] = dot(normed[...], wqkv[at : at + size, :], NT)
+    for piece in range(heads):
+        part = proj[:, piece * hd : (piece + 1) * hd]
+        inv = lax.rsqrt(jnp.sum(part * part, axis=-1, keepdims=True) * (1.0 / hd) + 1e-06)
+        raw[piece, :, :hd] = part
+        rms[piece] = inv
+        qh[piece] = jnp.zeros(qh.shape[1:], BF16)
+        qh[piece, :, :hd] = (part * inv).astype(BF16)
 
     slot_pick = (
         lax.broadcasted_iota(jnp.int32, (keep, keep), 0) == dest_ref[...]

time: 78.1 us -> 72.9 us (0.933)
  Pallas kernels: 73.2 us -> 67.5 us
    pallas_call x1, Pallas kernels: 73.2 us -> 67.5 us  [per_device(): pl.pallas_call(functools.partial(kernel, sizes), out_shape=(jax.ShapeDtyp...]
where the time goes in v3:
time: 72.9 us; the launch traced here: 72.2 us
  Pallas kernels  67.5 us (93%)
  local copies, waits for them, and re-layouts  4.04 us (6%)
    pallas_call x1, Pallas kernels, per_device(): pl.pallas_call(functools.partial(kernel, sizes), out_shape=(jax.ShapeDtyp...  67.5 us
    unnamed x2, local copies, waits for them, and re-layouts  4.04 us

profile of v3, /device:TPU:14, one launch (start us, length us, event | category | flops | bytes accessed | tf_op | source)
XLA Modules:
  0.0 72.2 jit_solution(11822564661581966845)
XLA Ops:
  0.6 67.5 %shard_map.113 = (bf16[256,1408]{1,0:T(8,128)(2,1)}, bf16[256,1408]{1,0:T(8,128)(2,1)}) custom-call(bf16[1024,1408]{1,0:T(8,128)(2,1)} %bitcast.9, s32[1,256]{1,0:T(1,128)} %bitcast.14, s32[1,256]{1,0:T(1,128)} %bitcast.15, s32[4,4]{1,0:T(4,128)} %counts_ref.1, s32[4,2,4]{2,1,0:T(2,128)} %bitcast.13, f32[1408]{0:T(1024)} %gain_ref.1, ...), custom_call_target="tpu_custom_call" | custom-call | tf_op jit(solution)/shard_map/pallas_call | solution.py:426
  68.1 2.0 %copy.14 = bf16[1,1,256,1408]{3,2,1,0:T(8,128)(2,1)} copy(bf16[1,1,256,1408]{3,2,1,0:T(8,128)(2,1)} %bitcast.11) | data formatting | bytes 1441792
  70.2 2.0 %copy.15 = bf16[1,1,256,1408]{3,2,1,0:T(8,128)(2,1)} copy(bf16[1,1,256,1408]{3,2,1,0:T(8,128)(2,1)} %bitcast.10) | data formatting | bytes 1441792
